TPU v7x, 32 devices: a whole 2x2x4 slice. The times are simulated.
32 devices in a mesh: gx: 4 (over z), gy: 4 (over y, x), gz: 2 (over core).
Axes of the slice: x: 2, y: 2, z: 4, core: 2. Of those that a mesh axis runs over, the one named last changes fastest.
Arguments:
- coeffs: float32 [5, 5, 5, 5, 512], P(None, None, None, None, ('gx', 'gy', 'gz')), may hold values from -6 to 6
- refine_flag: int32 [512], P(('gx', 'gy', 'gz')), may hold values from 0 to 1, as said below
- new_owner: int32 [512], P(('gx', 'gy', 'gz')), may hold values from 0 to 31, as said below
- inv_jac: float32 [5, 5, 5, 8192], P(None, None, None, ('gx', 'gy', 'gz')), may hold values from 0.02 to 0.2
- metric: float32 [3, 3, 5, 5, 5, 8192], P(None, None, None, None, None, ('gx', 'gy', 'gz')), may hold values from -3 to 3
- neighbor: int32 [4, 6, 8192], P(None, None, ('gx', 'gy', 'gz')), may hold values from 0 to 2047, as said below
- mortar: int32 [6, 8192], P(None, ('gx', 'gy', 'gz')), may hold values from 0 to 5, as said below
- export_up: int32 [8192], P(('gx', 'gy', 'gz')), may hold values from 0 to 1535, as said below
- export_down: int32 [8192], P(('gx', 'gy', 'gz')), may hold values from 0 to 1535, as said below
Outputs:
- rhs: float32 [5, 5, 5, 5, 8192], P(None, None, None, None, ('gx', 'gy', 'gz'))
Inputs may be any that keep to these rules, and one draw needn't show every extreme that they name: `new_owner`: device s keeps a middle run of its parents and sends a run at the head of its segment to devices s - 2 and s - 1 (the first parents to s - 2) and a run at the tail to s + 1 and s + 2 (the last parents to s + 2); no parent leaves the devices 0 to 32 - 1; at most 4 parents go from one device to one other device, and some device sends exactly 4 to each of s - 2, s - 1, s + 1, s + 2. `refine_flag`: the share of refined parents differs from device to device. `neighbor`: entries of used element slots name traces of used slots or halo entries; a slot that holds no element has kind 0; slots that a face's kind does not read hold any index. `mortar`: slots that hold no element have kind 0. `export_up`: entries name traces of used element slots. `export_down`: entries name traces of used element slots.
All inputs are finite; a program needn't handle non-finite values.
Results may differ from a plain program's by a relative error of at most 0.0003.
Values sent between devices are 32-bit elements; how exact they have to be, the bound alone decides.
A program may use at most 320 MiB of HBM per device.

v0:
```python
import jax
import jax.numpy as jnp
import numpy as np
from jax import lax
from jax.sharding import PartitionSpec as P

ORDER = 4


HIGHEST = lax.Precision.HIGHEST
mean_flow = (0.5, 0.3, 0.2)
speed_bound = 1.5
band_steps = (2, 1, -1, -2)


def from_behind(value, axis, steps):
    count = lax.axis_size(axis)
    first, last = (max(0, -steps), min(count, count - steps))
    return lax.ppermute(value, axis, [(source, source + steps) for source in range(first, last)])


def lobatto_rule(degree):
    count = degree + 1
    nodes = np.cos(np.pi * np.arange(count) / degree)
    table = np.zeros((count, count))
    for sweep in range(80):
        table[:, 0] = 1.0
        table[:, 1] = nodes
        for power in range(2, count):
            table[:, power] = (
                (2 * power - 1) * nodes * table[:, power - 1] - (power - 1) * table[:, power - 2]
            ) / power
        nodes = nodes - (nodes * table[:, degree] - table[:, degree - 1]) / (
            count * table[:, degree]
        )
    table[:, 0] = 1.0
    table[:, 1] = nodes
    for power in range(2, count):
        table[:, power] = (
            (2 * power - 1) * nodes * table[:, power - 1] - (power - 1) * table[:, power - 2]
        ) / power
    weights = 2.0 / (degree * count * table[:, degree] ** 2)
    return (np.array(nodes[::-1]), np.array(weights[::-1]))


def node_tables():
    degree = ORDER
    count = degree + 1
    nodes, weights = lobatto_rule(degree)
    bary = np.array(
        [
            1.0 / np.prod([nodes[k] - nodes[other] for other in range(count) if other != k])
            for k in range(count)
        ]
    )
    deriv = np.zeros((count, count))
    for row in range(count):
        for column in range(count):
            if row != column:
                deriv[row, column] = bary[column] / bary[row] / (nodes[row] - nodes[column])
        deriv[row, row] = -np.sum(deriv[row])
    interp = np.zeros((2, count, count))
    for half in range(2):
        points = (nodes + 2.0 * half - 1.0) / 2.0
        for column in range(count):
            value = np.ones(count)
            for other in range(count):
                if other != column:
                    value = value * (points - nodes[other]) / (nodes[column] - nodes[other])
            interp[half, :, column] = value
    project = (
        0.5 * np.transpose(interp, (0, 2, 1)) * weights[None, None, :] / weights[None, :, None]
    )
    return (
        jnp.asarray(deriv, jnp.float32),
        jnp.asarray(interp, jnp.float32),
        jnp.asarray(project, jnp.float32),
        float(1.0 / weights[0]),
    )


def refine_elements(parents, refined, interp):
    children = []
    for child in range(8):
        first, second, third = (child // 4, child // 2 % 2, child % 2)
        section = jnp.einsum("ak,vklme->valme", interp[first], parents, precision=HIGHEST)
        section = jnp.einsum("bl,valme->vabme", interp[second], section, precision=HIGHEST)
        section = jnp.einsum("cm,vabme->vabce", interp[third], section, precision=HIGHEST)
        if child == 0:
            section = jnp.where(refined, section, parents)
        else:
            section = jnp.where(refined, section, jnp.zeros_like(section))
        children.append(section)
    stacked = jnp.stack(children, axis=-1)
    return stacked.reshape(stacked.shape[:-2] + (stacked.shape[-2] * 8,))


def normal_flux(rows, state):
    along = rows[0] * state[1] + rows[1] * state[2] + rows[2] * state[3]
    carried = mean_flow[0] * rows[0] + mean_flow[1] * rows[1] + mean_flow[2] * rows[2]
    parts = [carried * state[0] + along]
    for direction in range(3):
        parts.append(carried * state[1 + direction] + rows[direction] * state[4])
    parts.append(carried * state[4] + along)
    return jnp.stack(parts)


def face_parts(array):
    return [
        array[:, 0],
        array[:, -1],
        array[:, :, 0],
        array[:, :, -1],
        array[:, :, :, 0],
        array[:, :, :, -1],
    ]


def face_traces(state):
    return jnp.concatenate(face_parts(state), axis=-1)


def apply_pair(left, right, traces):
    section = jnp.einsum("ak,vkle->vale", left, traces, precision=HIGHEST)
    return jnp.einsum("bl,vale->vabe", right, section, precision=HIGHEST)


def right_side(state, metric, inv_jac, neighbor, mortar, traces, before, after, tables):
    deriv, interp, project, lift_scale = tables
    count = state.shape[-1]
    volume = jnp.einsum("al,vlbce->vabce", deriv, normal_flux(metric[0], state), precision=HIGHEST)
    volume = volume + jnp.einsum(
        "bl,valce->vabce", deriv, normal_flux(metric[1], state), precision=HIGHEST
    )
    volume = volume + jnp.einsum(
        "cl,vable->vabce", deriv, normal_flux(metric[2], state), precision=HIGHEST
    )
    pieces = []
    for face in range(6):
        rows = face_parts(metric[face // 2])[face]
        pieces.append(rows if face % 2 == 1 else -rows)
    normals = jnp.concatenate(pieces, axis=-1)
    table = jnp.concatenate([traces, before, after], axis=-1)
    links = neighbor.reshape(4, 6 * count)
    kinds = mortar.reshape(6 * count)[None, None, None, :]
    gathered = [table[..., links[slot_number]] for slot_number in range(4)]
    outer = jnp.where(kinds == 0, gathered[0], jnp.zeros_like(gathered[0]))
    for kind in range(1, 5):
        fine = apply_pair(interp[(kind - 1) // 2], interp[(kind - 1) % 2], gathered[0])
        outer = outer + jnp.where(kinds == kind, fine, jnp.zeros_like(fine))
    coarse = apply_pair(project[0], project[0], gathered[0])
    for quarter in range(1, 4):
        coarse = coarse + apply_pair(project[quarter // 2], project[quarter % 2], gathered[quarter])
    outer = outer + jnp.where(kinds == 5, coarse, jnp.zeros_like(coarse))
    inner_flux = normal_flux(normals, traces)
    outer_flux = normal_flux(normals, outer)
    speed = speed_bound * (jnp.abs(normals[0]) + jnp.abs(normals[1]) + jnp.abs(normals[2]))
    upwind = 0.5 * (inner_flux + outer_flux) - 0.5 * speed * (outer - traces)
    lift = (upwind - inner_flux) * lift_scale
    volume = volume.at[:, 0].add(lift[..., 0:count])
    volume = volume.at[:, -1].add(lift[..., count : 2 * count])
    volume = volume.at[:, :, 0].add(lift[..., 2 * count : 3 * count])
    volume = volume.at[:, :, -1].add(lift[..., 3 * count : 4 * count])
    volume = volume.at[:, :, :, 0].add(lift[..., 4 * count : 5 * count])
    volume = volume.at[:, :, :, -1].add(lift[..., 5 * count : 6 * count])
    return -inv_jac * volume


def assemble(bands, own):
    return jnp.concatenate([bands[0], bands[1], own, bands[2], bands[3]], axis=-1)


def move_children(outgoing, width):
    received = []
    for number in range(4):
        piece = outgoing[..., number * width : (number + 1) * width]
        received.append(from_behind(piece, ("gx", "gy", "gz"), band_steps[number]))
    return received


def local(
    coeffs, refine_flag, new_owner, inv_jac, metric, neighbor, mortar, export_up, export_down
):
    tables = node_tables()
    count = coeffs.shape[-1]
    width = count // 4
    rank_here = lax.axis_index(("gx", "gy", "gz"))
    position = jnp.arange(count, dtype=jnp.int32)
    same = new_owner[:, None] == new_owner[None, :]
    earlier = position[None, :] < position[:, None]
    slot = jnp.sum((same & earlier).astype(jnp.int32), axis=1)
    delta = new_owner - rank_here
    staying = delta == 0
    own = jnp.where(staying[None, None, None, None, :], coeffs, jnp.zeros_like(coeffs))
    own_flags = jnp.where(staying, refine_flag, jnp.zeros_like(refine_flag))
    band = jnp.where(delta > 0, 2 - delta, 1 - delta)
    outgoing_spot = jnp.where(staying, 4 * width, band * width + slot)
    outgoing = (
        jnp.zeros(coeffs.shape[:-1] + (4 * width,), jnp.float32)
        .at[..., outgoing_spot]
        .set(coeffs, mode="drop")
    )
    out_flags = jnp.zeros((4 * width,), jnp.int32).at[outgoing_spot].set(refine_flag, mode="drop")
    out_children = refine_elements(outgoing, out_flags > 0, tables[1])
    own_children = refine_elements(own, own_flags > 0, tables[1])
    received = move_children(out_children, 8 * width)
    state = assemble(received, own_children)
    traces = face_traces(state)
    before = from_behind(traces[..., export_up], ("gx", "gy", "gz"), 1)
    after = from_behind(traces[..., export_down], ("gx", "gy", "gz"), -1)
    return right_side(state, metric, inv_jac, neighbor, mortar, traces, before, after, tables)


def solution(mesh):
    in_specs = (
        P(None, None, None, None, ("gx", "gy", "gz")),
        P(("gx", "gy", "gz")),
        P(("gx", "gy", "gz")),
        P(None, None, None, ("gx", "gy", "gz")),
        P(None, None, None, None, None, ("gx", "gy", "gz")),
        P(None, None, ("gx", "gy", "gz")),
        P(None, ("gx", "gy", "gz")),
        P(("gx", "gy", "gz")),
        P(("gx", "gy", "gz")),
    )
    out_specs = P(None, None, None, None, ("gx", "gy", "gz"))
    return jax.shard_map(local, mesh=mesh, in_specs=in_specs, out_specs=out_specs, check_vma=False)
```

profile of v0, /device:TPU:24, one launch (start us, length us, event | category | flops | bytes accessed | tf_op | source)
XLA Modules:
  0.0 391.9 jit_solution(11656583830608220492)
XLA Ops:
  0.9 1.9 copy.176
  17.0 1.4 fusion.26
  22.7 6.7 %copy.272 = f32[5,5,5,5,16,8]{5,4,1,2,0,3:T(8,128)} copy(f32[5,5,5,5,16,8]{4,3,2,1,0,5:T(8,128)} %fusion.20) | data formatting | bytes 640000 | tf_op jit(solution)/shard_map/reshape | solution.py:95
  29.5 4.4 %reshape.674 = f32[5,5,5,5,128]{4,1,2,0,3:T(8,128)S(1)} reshape(f32[5,5,5,5,16,8]{5,4,1,2,0,3:T(8,128)} %copy.272) | data formatting | bytes 640000 | tf_op jit(solution)/shard_map/reshape | solution.py:95
  33.9 1.7 fusion.185
  35.6 3.3 collective-permute-start
  38.9 1.9 collective-permute-start.1
  40.8 5.4 %collective-permute-start.2 = (f32[5,5,5,5,32]{4,1,2,0,3:T(8,128)}, f32[5,5,5,5,32]{4,1,2,0,3:T(8,128)}, u32[]{:S(2)}, u32[]{:S(2)}) collective-permute-start(f32[5,5,5,5,32]{4,1,2,0,3:T(8,128)} %get-tuple-element.132), channel_id=1, source_target_pairs={{1,0},{2,1},{3,2},{4,3},{5,4},{6,5},{7,6},{8,7},{9,8},{10,9},{11,1... | collective-permute-start | bytes 240008 | tf_op jit(solution)/shard_map/ppermute | solution.py:19
  46.3 2.7 collective-permute-start.3
  53.1 1.7 fusion.181
  60.4 1.4 fusion.9
  61.9 1.4 fusion.7
  66.2 6.9 %copy.271 = f32[5,5,5,5,16,8]{5,4,1,2,0,3:T(8,128)} copy(f32[5,5,5,5,16,8]{4,3,2,1,0,5:T(8,128)} %fusion.3) | data formatting | bytes 640000 | tf_op jit(solution)/shard_map/reshape | solution.py:95
  73.1 4.4 %reshape.673 = f32[5,5,5,5,128]{4,1,2,0,3:T(8,128)S(1)} reshape(f32[5,5,5,5,16,8]{5,4,1,2,0,3:T(8,128)} %copy.271) | data formatting | bytes 640000 | tf_op jit(solution)/shard_map/reshape | solution.py:95
  79.9 2.4 concatenate.25
  87.1 14.7 %copy.230 = f32[5,5,5,1536]{2,1,3,0:T(8,128)} copy(f32[5,5,5,1536]{3,1,2,0:T(8,128)S(1)} %get-tuple-element.104) | data formatting | bytes 1536000 | tf_op jit(solution)/shard_map/concatenate | solution.py:120
  101.8 13.5 %gather_fusion = f32[256,5,5,5]{3,2,1,0:T(8,128)} fusion(f32[5,5,5,1536]{2,1,3,0:T(8,128)} %copy.230, s32[1024]{0:T(1024)S(1)} %pad_clamp_fusion.5), kind=kCustom, calls=%fused_computation | custom fusion | bytes 257024 | tf_op jit(solution)/shard_map/gather | solution.py:209
  115.3 4.0 %copy.231 = f32[256,5,5,5]{0,2,3,1:T(8,128)} copy(f32[256,5,5,5]{3,2,1,0:T(8,128)} %gather_fusion) | data formatting | bytes 256000 | tf_op jit(solution)/shard_map/gather | solution.py:209
  119.3 1.9 collective-permute-start.4
  121.2 13.5 %gather_fusion.1 = f32[256,5,5,5]{3,2,1,0:T(8,128)} fusion(f32[5,5,5,1536]{2,1,3,0:T(8,128)} %copy.230, s32[1024]{0:T(1024)S(1)} %pad_clamp_fusion.4), kind=kCustom, calls=%fused_computation.1 | custom fusion | bytes 257024 | tf_op jit(solution)/shard_map/gather | solution.py:210
  134.8 4.0 %copy.233 = f32[256,5,5,5]{0,2,3,1:T(8,128)} copy(f32[256,5,5,5]{3,2,1,0:T(8,128)} %gather_fusion.1) | data formatting | bytes 256000 | tf_op jit(solution)/shard_map/gather | solution.py:210
  138.8 5.6 %collective-permute-start.5 = (f32[5,5,5,256]{3,1,2,0:T(8,128)}, f32[5,5,5,256]{3,1,2,0:T(8,128)S(1)}, u32[]{:S(2)}, u32[]{:S(2)}) collective-permute-start(f32[5,5,5,256]{3,1,2,0:T(8,128)} %bitcast.635), channel_id=1, source_target_pairs={{1,0},{2,1},{3,2},{4,3},{5,4},{6,5},{7,6},{8,7},{9,8},{10,9},{11,1... | collective-permute-start | bytes 384008 | tf_op jit(solution)/shard_map/ppermute | solution.py:19
  150.3 2.4 fusion.1
  152.7 1.7 constant_dynamic-update-slice_fusion.7
  155.1 20.5 %copy.234 = f32[5,5,5,2048]{2,1,3,0:T(8,128)} copy(f32[5,5,5,2048]{3,1,2,0:T(8,128)} %constant_dynamic-update-slice_fusion.6) | data formatting | bytes 2048000 | tf_op jit(solution)/shard_map/concatenate | solution.py:143
  175.6 22.5 %gather_fusion.2 = f32[1536,5,5,5]{3,2,1,0:T(8,128)} fusion(f32[5,5,5,2048]{2,1,3,0:T(8,128)} %copy.234, s32[2048]{0:T(1024)S(1)} %get-tuple-element.163), kind=kCustom, calls=%fused_computation.2 | custom fusion | bytes 1542144 | tf_op jit(solution)/shard_map/gather | solution.py:146
  198.1 16.8 %copy.235 = f32[1536,5,5,5]{0,2,3,1:T(8,128)S(1)} copy(f32[1536,5,5,5]{3,2,1,0:T(8,128)} %gather_fusion.2) | data formatting | bytes 1536000 | tf_op jit(solution)/shard_map/gather | solution.py:146
  216.1 2.7 fusion.48
  218.8 2.7 fusion.50
  222.7 2.7 fusion.52
  225.3 2.7 fusion.54
  228.0 22.7 %gather_fusion.5 = f32[1536,5,5,5]{3,2,1,0:T(8,128)} fusion(f32[5,5,5,2048]{2,1,3,0:T(8,128)} %copy.234, s32[2048]{0:T(1024)S(1)} %get-tuple-element.160), kind=kCustom, calls=%fused_computation.5 | custom fusion | bytes 1542144 | tf_op jit(solution)/shard_map/gather | solution.py:146
  250.7 17.7 %copy.255 = f32[5,5,5,1536]{3,1,2,0:T(8,128)} copy(f32[5,5,5,1536]{2,1,0,3:T(8,128)} %bitcast.625) | data formatting | bytes 1536000 | tf_op jit(solution)/shard_map/gather | solution.py:146
  268.4 2.5 convolution_bitcast_fusion
  270.9 2.7 fusion.40
  273.6 22.5 %gather_fusion.4 = f32[1536,5,5,5]{3,2,1,0:T(8,128)} fusion(f32[5,5,5,2048]{2,1,3,0:T(8,128)} %copy.234, s32[2048]{0:T(1024)S(1)} %get-tuple-element.161), kind=kCustom, calls=%fused_computation.4 | custom fusion | bytes 1542144 | tf_op jit(solution)/shard_map/gather | solution.py:146
  296.1 17.7 %copy.251 = f32[5,5,5,1536]{3,1,2,0:T(8,128)} copy(f32[5,5,5,1536]{2,1,0,3:T(8,128)} %bitcast.626) | data formatting | bytes 1536000 | tf_op jit(solution)/shard_map/gather | solution.py:146
  313.8 2.5 convolution_bitcast_fusion.1
  316.3 2.3 convolution_bitcast_fusion.3
  318.6 2.7 fusion.42
  321.3 22.5 %gather_fusion.3 = f32[1536,5,5,5]{3,2,1,0:T(8,128)} fusion(f32[5,5,5,2048]{2,1,3,0:T(8,128)} %copy.234, s32[2048]{0:T(1024)S(1)} %get-tuple-element.162), kind=kCustom, calls=%fused_computation.3 | custom fusion | bytes 1542144 | tf_op jit(solution)/shard_map/gather | solution.py:146
  343.8 17.9 %copy.246 = f32[5,5,5,1536]{3,1,2,0:T(8,128)} copy(f32[5,5,5,1536]{2,1,0,3:T(8,128)} %bitcast.624) | data formatting | bytes 1536000 | tf_op jit(solution)/shard_map/gather | solution.py:146
  361.7 2.6 convolution_bitcast_fusion.2
  364.3 1.6 fusion.44
  365.9 3.0 fusion.46
  369.0 5.9 %bitcast_add_fusion = f32[5,5,5,1536]{3,1,2,0:T(8,128)S(1)} fusion(f32[1536,5,5,5]{0,2,3,1:T(8,128)S(1)} %copy.235, f32[5,5,1536,5]{2,3,1,0:T(8,128)S(1)} %copy-done.6, f32[5,5,1536,5]{2,3,1,0:T(8,128)S(1)} %copy-done.7, f32[5,5,1536,5]{2,3,1,0:T(8,128)S(1)} %fusion.44, f32[5,5,1536,5]{2,3,1,0:T(8,128)S(1)} %fusion.46, f32[5,5,1536,5]{2,3,1,0:T(8,128)S(1)} %copy-done.2, ...), kind=kLoop, calls=%fused_computation.79 | loop fusion | flops 2688000 | bytes 7689216 | tf_op jit(solution)/shard_map/add | solution.py:154
  378.1 5.0 %scatter-add.20 = f32[5,5,5,5,256]{4,1,2,0,3:T(8,128)S(1)} dynamic-update-slice(f32[5,5,5,5,256]{4,1,2,0,3:T(8,128)S(1)} %copy-done, f32[5,1,5,5,256]{4,1,2,0,3:T(1,128)S(1)} %slice_add_fusion.3, s32[]{:T(128)} %constant.204.clone.1, s32[]{:T(128)} %constant.204.clone.1, s32[]{:T(128)} %constant.204.clone.1, s32[]{:T(128)} %constant.204.clone.1, s32[]{:T(128)} %constant.204.clone.1) | dynamic-update-slice | bytes 256004 | tf_op jit(solution)/shard_map/scatter-add | solution.py:160
  383.3 5.0 %scatter-add.21 = f32[5,5,5,5,256]{4,1,2,0,3:T(8,128)S(1)} dynamic-update-slice(f32[5,5,5,5,256]{4,1,2,0,3:T(8,128)S(1)} %scatter-add.20, f32[5,1,5,5,256]{4,1,2,0,3:T(1,128)S(1)} %slice_add_fusion.2, s32[]{:T(128)} %constant.204.clone.1, s32[]{:T(128)} %constant.211.clone.1, s32[]{:T(128)} %constant.204.clone.1, s32[]{:T(128)} %constant.204.clone.1, s32[]{:T(128)} %constant.204.clone.1) | dynamic-update-slice | bytes 256004 | tf_op jit(solution)/shard_map/scatter-add | solution.py:161
  (170 shorter events, 54.4 us)
Async XLA Ops:
  0.0 2.8 copy-start.28
  5.8 0.9 copy-start.18
  6.7 1.2 copy-start.17
  9.1 1.2 copy-start.31
  33.9 15.1 %copy-start.15 = (f32[5,5,5,5,16]{4,3,2,1,0:T(8,128)S(1)}, f32[5,5,5,5,16]{4,3,2,1,0:T(8,128)}, u32[]{:S(2)}) copy-start(f32[5,5,5,5,16]{4,3,2,1,0:T(8,128)} %param.24) | copy-start | bytes 120004
  35.6 44.3 %collective-permute-start = (f32[5,5,5,5,32]{4,1,2,0,3:T(8,128)}, f32[5,5,5,5,32]{4,1,2,0,3:T(8,128)}, u32[]{:S(2)}, u32[]{:S(2)}) collective-permute-start(f32[5,5,5,5,32]{4,1,2,0,3:T(8,128)} %get-tuple-element.134), channel_id=1, source_target_pairs={{0,2},{1,3},{2,4},{3,5},{4,6},{5,7},{6,8},{7,9},{8,10},{9,11},{10,... | collective-permute-start | bytes 240008 | tf_op jit(solution)/shard_map/ppermute | solution.py:19
  38.9 41.0 %collective-permute-start.1 = (f32[5,5,5,5,32]{4,1,2,0,3:T(8,128)}, f32[5,5,5,5,32]{4,1,2,0,3:T(8,128)}, u32[]{:S(2)}, u32[]{:S(2)}) collective-permute-start(f32[5,5,5,5,32]{4,1,2,0,3:T(8,128)} %get-tuple-element.133), channel_id=1, source_target_pairs={{0,1},{1,2},{2,3},{3,4},{4,5},{5,6},{6,7},{7,8},{8,9},{9,10},{10,1... | collective-permute-start | bytes 240008 | tf_op jit(solution)/shard_map/ppermute | solution.py:19
  40.8 39.1 %collective-permute-start.2 = (f32[5,5,5,5,32]{4,1,2,0,3:T(8,128)}, f32[5,5,5,5,32]{4,1,2,0,3:T(8,128)}, u32[]{:S(2)}, u32[]{:S(2)}) collective-permute-start(f32[5,5,5,5,32]{4,1,2,0,3:T(8,128)} %get-tuple-element.132), channel_id=1, source_target_pairs={{1,0},{2,1},{3,2},{4,3},{5,4},{6,5},{7,6},{8,7},{9,8},{10,9},{11,1... | collective-permute-start | bytes 240008 | tf_op jit(solution)/shard_map/ppermute | solution.py:19
  46.3 33.7 %collective-permute-start.3 = (f32[5,5,5,5,32]{4,1,2,0,3:T(8,128)}, f32[5,5,5,5,32]{4,1,2,0,3:T(8,128)}, u32[]{:S(2)}, u32[]{:S(2)}) collective-permute-start(f32[5,5,5,5,32]{4,1,2,0,3:T(8,128)} %get-tuple-element.131), channel_id=1, source_target_pairs={{2,0},{3,1},{4,2},{5,3},{6,4},{7,5},{8,6},{9,7},{10,8},{11,9},{12,... | collective-permute-start | bytes 240008 | tf_op jit(solution)/shard_map/ppermute | solution.py:19
  51.5 1.4 copy-start.8
  73.1 4.5 %copy-start.29 = (s32[256]{0:T(256)S(1)}, s32[256]{0:T(256)}, u32[]{:S(2)}) copy-start(s32[256]{0:T(256)} %param.32) | copy-start | bytes 3076
  73.1 4.5 %copy-start.30 = (s32[256]{0:T(256)S(1)}, s32[256]{0:T(256)}, u32[]{:S(2)}) copy-start(s32[256]{0:T(256)} %param.31) | copy-start | bytes 3076
  73.1 4.5 %copy-start.24 = (s32[4,6,256]{2,0,1:T(4,128)S(1)}, s32[4,6,256]{2,0,1:T(4,128)}, u32[]{:S(2)}) copy-start(s32[4,6,256]{2,0,1:T(4,128)} %param.29) | copy-start | bytes 73732
  73.1 4.7 %copy-start.26 = (s32[6,256]{1,0:T(8,128)S(1)}, s32[6,256]{1,0:T(8,128)}, u32[]{:S(2)}) copy-start(s32[6,256]{1,0:T(8,128)} %param.30) | copy-start | bytes 18436
  78.2 0.9 copy-start.19
  119.3 33.4 %collective-permute-start.4 = (f32[5,5,5,256]{3,1,2,0:T(8,128)}, f32[5,5,5,256]{3,1,2,0:T(8,128)}, u32[]{:S(2)}, u32[]{:S(2)}) collective-permute-start(f32[5,5,5,256]{3,1,2,0:T(8,128)} %bitcast.634), channel_id=1, source_target_pairs={{0,1},{1,2},{2,3},{3,4},{4,5},{5,6},{6,7},{7,8},{8,9},{9,10},{10,1... | collective-permute-start | bytes 384008 | tf_op jit(solution)/shard_map/ppermute | solution.py:19
  138.7 7.0 %copy-start.9 = (f32[1,1,5,5,5,256]{5,1,4,3,2,0:T(1,128)S(1)}, f32[1,1,5,5,5,256]{5,1,4,3,2,0:T(1,128)}, u32[]{:S(2)}) copy-start(f32[1,1,5,5,5,256]{5,1,4,3,2,0:T(1,128)} %get-tuple-element.97) | copy-start | bytes 384004
  138.7 7.0 %copy-start.10 = (f32[1,1,5,5,5,256]{5,1,4,3,2,0:T(1,128)S(1)}, f32[1,1,5,5,5,256]{5,1,4,3,2,0:T(1,128)}, u32[]{:S(2)}) copy-start(f32[1,1,5,5,5,256]{5,1,4,3,2,0:T(1,128)} %get-tuple-element.98) | copy-start | bytes 384004
  138.8 7.0 %copy-start.12 = (f32[1,1,5,5,5,256]{5,1,4,3,2,0:T(1,128)S(1)}, f32[1,1,5,5,5,256]{5,1,4,3,2,0:T(1,128)}, u32[]{:S(2)}) copy-start(f32[1,1,5,5,5,256]{5,1,4,3,2,0:T(1,128)} %get-tuple-element.91) | copy-start | bytes 384004
  138.8 7.0 %copy-start.13 = (f32[1,1,5,5,5,256]{5,1,4,3,2,0:T(1,128)S(1)}, f32[1,1,5,5,5,256]{5,1,4,3,2,0:T(1,128)}, u32[]{:S(2)}) copy-start(f32[1,1,5,5,5,256]{5,1,4,3,2,0:T(1,128)} %get-tuple-element.94) | copy-start | bytes 384004
  138.8 7.0 %copy-start.14 = (f32[1,1,5,5,5,256]{5,1,4,3,2,0:T(1,128)S(1)}, f32[1,1,5,5,5,256]{5,1,4,3,2,0:T(1,128)}, u32[]{:S(2)}) copy-start(f32[1,1,5,5,5,256]{5,1,4,3,2,0:T(1,128)} %get-tuple-element.95) | copy-start | bytes 384004
  138.8 15.6 %collective-permute-start.5 = (f32[5,5,5,256]{3,1,2,0:T(8,128)}, f32[5,5,5,256]{3,1,2,0:T(8,128)S(1)}, u32[]{:S(2)}, u32[]{:S(2)}) collective-permute-start(f32[5,5,5,256]{3,1,2,0:T(8,128)} %bitcast.635), channel_id=1, source_target_pairs={{1,0},{2,1},{3,2},{4,3},{5,4},{6,5},{7,6},{8,7},{9,8},{10,9},{11,1... | collective-permute-start | bytes 384008 | tf_op jit(solution)/shard_map/ppermute | solution.py:19
  145.7 0.9 copy-start.11
  147.2 0.7 copy-start.25
  149.1 1.2 copy-start.27
  198.1 16.8 %copy-start.23 = (f32[5,5,1,1]{1,0,3,2:T(8,128)S(1)}, f32[5,5,1,1]{1,0,3,2:T(8,128)}, u32[]{:S(2)}) copy-start(f32[5,5,1,1]{1,0,3,2:T(8,128)} %constant.238) | copy-start | bytes 304
  216.1 2.7 copy-start.22
  250.7 17.7 %copy-start.21 = (f32[5,5,1,1]{1,0,3,2:T(8,128)S(1)}, f32[5,5,1,1]{1,0,3,2:T(8,128)}, u32[]{:S(2)}) copy-start(f32[5,5,1,1]{1,0,3,2:T(8,128)} %constant.240) | copy-start | bytes 304
  313.8 2.5 copy-start.20
  361.7 7.3 %copy-start.6 = (f32[5,5,1536,5]{2,3,1,0:T(8,128)S(1)}, f32[5,5,1536,5]{2,3,1,0:T(8,128)}, u32[]{:S(2)}) copy-start(f32[5,5,1536,5]{2,3,1,0:T(8,128)} %fusion.40) | copy-start | bytes 2304004
  361.7 7.3 %copy-start.7 = (f32[5,5,1536,5]{2,3,1,0:T(8,128)S(1)}, f32[5,5,1536,5]{2,3,1,0:T(8,128)}, u32[]{:S(2)}) copy-start(f32[5,5,1536,5]{2,3,1,0:T(8,128)} %fusion.42) | copy-start | bytes 2304004
  364.3 4.7 %copy-start.4 = (f32[5,5,1536,5]{2,3,1,0:T(8,128)S(1)}, f32[5,5,1536,5]{2,3,1,0:T(8,128)}, u32[]{:S(2)}) copy-start(f32[5,5,1536,5]{2,3,1,0:T(8,128)} %fusion.52) | copy-start | bytes 2304004
  364.3 4.7 %copy-start.5 = (f32[5,5,1536,5]{2,3,1,0:T(8,128)S(1)}, f32[5,5,1536,5]{2,3,1,0:T(8,128)}, u32[]{:S(2)}) copy-start(f32[5,5,1536,5]{2,3,1,0:T(8,128)} %fusion.54) | copy-start | bytes 2304004
  365.9 3.1 copy-start.2
  365.9 3.1 copy-start.3
  376.2 1.1 copy-start.1
  376.2 1.7 copy-start
  388.3 2.1 copy-start.16
where the time goes:
time: 399 us; the launch traced here: 392 us
  local copies, waits for them, and re-layouts  289 us (72%)
  matrix products  67.4 us (17%)
  starting transfers between devices  20.8 us (5%)
  other arithmetic  13.6 us (3%)
    gather x8, local copies, waits for them, and re-layouts, right_side(): gathered = [table[..., links[slot_number]] for slot_number in range(4)]  160 us
    dot_general x16, matrix products, refine_elements(): jnp.einsum('cm,vabme->vabce', interp[third], section, precision=HIGHEST)  22.7 us
    reshape x4, local copies, waits for them, and re-layouts, refine_elements(): return stacked.reshape(stacked.shape[:-2] + (stacked.shape[-2] * 8,))  22.5 us
    concatenate x2, local copies, waits for them, and re-layouts, right_side(): table = jnp.concatenate([traces, before, after], axis=-1)  21.2 us
    ppermute x6, starting transfers between devices, from_behind(): lax.ppermute(value, axis, [(source, source + steps) for source in range(f...  20.8 us
    dot_general x8, matrix products, apply_pair(): return jnp.einsum('bl,vale->vabe', right, section, precision=HIGHEST)  20.7 us
    gather x2, local copies, waits for them, and re-layouts, local(): after = from_behind(traces[..., export_down], ('gx', 'gy', 'gz'), -1)  17.5 us
    gather x2, local copies, waits for them, and re-layouts, local(): before = from_behind(traces[..., export_up], ('gx', 'gy', 'gz'), 1)  17.5 us
  transfers between devices with their start and end apart: 6, of which 0 were waited for; matrix products, arithmetic and copies ran while one was open for 14% of the time, Pallas kernels for 0%

commit v1 on v0

v1 whole, which is shorter than its diff:
```python
import functools

import jax
import jax.numpy as jnp
import ml_dtypes
import numpy as np
from jax import lax
from jax.experimental import pallas as pl
from jax.experimental.pallas import tpu as pltpu
from jax.sharding import PartitionSpec as P

ORDER = 4
NP = ORDER + 1
AXES = ("gx", "gy", "gz")
mean_flow = (0.5, 0.3, 0.2)
speed_bound = 1.5
band_steps = (2, 1, -1, -2)
F32 = jnp.float32
BF16 = jnp.bfloat16
MESH = pl.DeviceIdType.MESH


def lobatto_rule(degree):
    count = degree + 1
    nodes = np.cos(np.pi * np.arange(count) / degree)
    table = np.zeros((count, count))

    def fill():
        table[:, 0] = 1.0
        table[:, 1] = nodes
        for power in range(2, count):
            table[:, power] = (
                (2 * power - 1) * nodes * table[:, power - 1] - (power - 1) * table[:, power - 2]
            ) / power

    for sweep in range(80):
        fill()
        nodes = nodes - (nodes * table[:, degree] - table[:, degree - 1]) / (
            count * table[:, degree]
        )
    fill()
    weights = 2.0 / (degree * count * table[:, degree] ** 2)
    return (np.array(nodes[::-1]), np.array(weights[::-1]))


def node_tables():
    count = NP
    nodes, weights = lobatto_rule(ORDER)
    bary = np.array(
        [
            1.0 / np.prod([nodes[k] - nodes[other] for other in range(count) if other != k])
            for k in range(count)
        ]
    )
    deriv = np.zeros((count, count))
    for row in range(count):
        for column in range(count):
            if row != column:
                deriv[row, column] = bary[column] / bary[row] / (nodes[row] - nodes[column])
        deriv[row, row] = -np.sum(deriv[row])
    interp = np.zeros((2, count, count))
    for half in range(2):
        points = (nodes + 2.0 * half - 1.0) / 2.0
        for column in range(count):
            value = np.ones(count)
            for other in range(count):
                if other != column:
                    value = value * (points - nodes[other]) / (nodes[column] - nodes[other])
            interp[half, :, column] = value
    project = (
        0.5 * np.transpose(interp, (0, 2, 1)) * weights[None, None, :] / weights[None, :, None]
    )
    return deriv, interp, project, float(1.0 / weights[0])


def split_np(array):
    array = np.asarray(array, np.float32)
    high = array.astype(ml_dtypes.bfloat16)
    low = (array - high.astype(np.float32)).astype(ml_dtypes.bfloat16)
    return high, low


def widen(matrix, rows=True, columns=True):
    block = matrix.reshape(25, 5, 25, 5)
    full = np.zeros((25, 8, 25, 8))
    full[:, :5, :, :5] = block
    return full.reshape(200, 200)


def operators():
    deriv, interp, project, lift_scale = node_tables()
    eye = np.eye(NP)
    kron3 = lambda x, y, z: np.kron(np.kron(x, y), z)
    refine = np.zeros((256, 8 * 256))
    for child in range(8):
        h = (child // 4, child // 2 % 2, child % 2)
        whole = widen(kron3(interp[h[0]], interp[h[1]], interp[h[2]]))
        refine[:200, child * 256 : child * 256 + 200] = whole.T
    slope = np.concatenate(
        [
            widen(kron3(deriv, eye, eye)),
            widen(kron3(eye, deriv, eye)),
            widen(kron3(eye, eye, deriv)),
        ],
        axis=1,
    )
    pick = np.zeros((6 * 32, 200))
    for face in range(6):
        for m1 in range(NP):
            for m2 in range(NP):
                end = ORDER * (face % 2)
                node = [(end, m1, m2), (m1, end, m2), (m1, m2, end)][face // 2]
                pick[face * 32 + m1 * NP + m2, (node[0] * 5 + node[1]) * 8 + node[2]] = 1.0
    pairs = [np.kron(eye, eye)]
    pairs += [np.kron(interp[k // 2], interp[k % 2]) for k in range(4)]
    pairs += [np.kron(project[k // 2], project[k % 2]) for k in range(4)]
    mortar = np.zeros((9 * 160, 128))
    for number, pair in enumerate(pairs):
        for v in range(5):
            top = number * 160 + v * 32
            mortar[top : top + 25, v * 25 : v * 25 + 25] = pair
    mortar_high, mortar_low = split_np(mortar)
    mortar_twice = np.concatenate([mortar_high, mortar_high], axis=1)
    spread = lambda x: x.astype(ml_dtypes.bfloat16)
    arrays = (
        *split_np(refine),
        *split_np(slope),
        spread(pick),
        spread(pick.T.copy()),
        mortar_twice,
        mortar_low,
    )
    return arrays, lift_scale


def split(value):
    high = value.astype(BF16)
    return high, (value - high.astype(F32)).astype(BF16)


def dot(left, right):
    return jnp.dot(left, right, preferred_element_type=F32)


def one_hot(index, chunks):
    count = index.shape[1]
    rows = lax.broadcasted_iota(jnp.int32, (256, count), 0)
    parts = []
    for chunk in range(chunks):
        parts.append(
            jnp.where(rows == index - chunk * 256, 1.0, 0.0).astype(BF16)
        )
    return jnp.concatenate(parts, axis=0)


def body(
    sizes,
    lift_scale,
    coeffs_ref,
    flag_ref,
    owner_ref,
    jac_ref,
    metric_ref,
    near_ref,
    kind_ref,
    up_ref,
    down_ref,
    refine_hi,
    refine_lo,
    slope_hi,
    slope_lo,
    pick,
    pick_t,
    mortar_hi,
    mortar_lo,
    out_ref,
    packed,
    leaving,
    arriving,
    state,
    rows_of,
    flux_hi,
    flux_lo,
    volume,
    inner,
    normal,
    flat,
    table,
    sending,
    halo,
    lift,
    send_sem,
    recv_sem,
):
    nx, ny, nz = sizes
    total = nx * ny * nz
    rank = (lax.axis_index("gx") * ny + lax.axis_index("gy")) * nz + lax.axis_index("gz")

    def place(steps):
        other = lax.rem(rank + steps + total, total)
        return (other // (ny * nz), lax.rem(other // nz, ny), lax.rem(other, nz))

    barrier = pltpu.get_barrier_semaphore()
    for steps in band_steps:
        pl.semaphore_signal(barrier, inc=1, device_id=place(steps), device_id_type=MESH)

    count = coeffs_ref.shape[-1]
    packed[...] = jnp.zeros_like(packed)
    for block in range(125):
        v, ab = divmod(block, 25)
        packed[pl.ds(v * 256 + ab * 8, 5), :] = coeffs_ref[block]
    owner = jnp.broadcast_to(owner_ref[...], (count, count))
    first = lax.broadcasted_iota(jnp.int32, (count, count), 0)
    second = lax.broadcasted_iota(jnp.int32, (count, count), 1)
    column = jnp.sum(jnp.where(first == second, owner, 0), axis=1, keepdims=True)
    slot = jnp.sum(
        jnp.where((column == owner) & (first < second), 1, 0), axis=0, keepdims=True
    )
    delta = owner_ref[...] - rank
    band = jnp.where(delta > 0, 2 - delta, 1 - delta)
    own_place = 32 + lax.broadcasted_iota(jnp.int32, (1, count), 1)
    spot = jnp.where(delta == 0, own_place, band * 8 + slot)
    slots = 32 + count
    chosen = jnp.where(
        lax.broadcasted_iota(jnp.int32, (slots, count), 0) == spot, 1.0, 0.0
    ).astype(F32)
    placed = lax.dot_general(
        chosen,
        packed[...],
        (((1,), (1,)), ((), ())),
        precision=lax.Precision.HIGHEST,
        preferred_element_type=F32,
    )
    flags = jnp.sum(chosen * flag_ref[...].astype(F32), axis=1, keepdims=True)
    flags = jnp.broadcast_to(flags, (slots, 128))
    for k in range(4):
        leaving[k, :, 0:1280] = placed[k * 8 : k * 8 + 8]
        leaving[k, :, 1280:1408] = flags[k * 8 : k * 8 + 8]

    pl.semaphore_wait(barrier, 4)
    moves = []
    for k in range(4):
        move = pltpu.make_async_remote_copy(
            src_ref=leaving.at[k],
            dst_ref=arriving.at[k],
            send_sem=send_sem.at[k],
            recv_sem=recv_sem.at[k],
            device_id=place(band_steps[k]),
            device_id_type=MESH,
        )
        move.start()
        moves.append(move)

    rows_of[...] = jnp.zeros_like(rows_of)
    for i in range(3):
        for j in range(3):
            rows_of[i, :, 0:5, j * 256 : j * 256 + 256] = metric_ref[
                i * 25 : i * 25 + 25, :, j, :
            ]
    for i in range(3):
        high, low = split(rows_of[i].reshape(200, 768))
        faces = pick[i * 64 : i * 64 + 64, :]
        normal[i * 64 : i * 64 + 64, :] = dot(faces, high) + dot(faces, low)
    for move in moves:
        move.wait()

    parents = [
        jnp.concatenate(
            [arriving[k, :, v * 256 : v * 256 + 256] for k in range(4)]
            + [placed[32:, v * 256 : v * 256 + 256]],
            axis=0,
        )
        for v in range(5)
    ]
    high, low = split(jnp.concatenate(parents, axis=0))
    spread = dot(high, refine_hi[...]) + dot(low, refine_hi[...]) + dot(high, refine_lo[...])
    refined = jnp.concatenate([arriving[k, :, 1280:1281] for k in range(4)] + [flags[32:, 0:1]], axis=0)
    row = lax.broadcasted_iota(jnp.int32, (slots, 256), 0)
    lane = lax.broadcasted_iota(jnp.int32, (slots, 256), 1)
    number, within = row >> 3, row & 7
    width = count // 4
    far = jnp.where(number < 2, number * width, count + number * width) + within
    far = jnp.where(within < width, far, -1000)
    base = 8 * jnp.where(row >= 32, 2 * width + row - 32, far)
    routes = [jnp.where(lane == base + child, refined, 0.0) for child in range(8)]
    routes.append(jnp.where(lane == base, 1.0 - refined, 0.0))
    route = jnp.concatenate(routes, axis=0).astype(BF16)
    over = (((0,), (0,)), ((), ()))
    for v in range(5):
        pieces = [spread[v * slots : (v + 1) * slots, c * 256 : c * 256 + 256] for c in range(8)]
        stacked = jnp.concatenate(pieces + [parents[v]], axis=0)
        high, low = split(stacked)
        value = lax.dot_general(high, route, over, preferred_element_type=F32)
        value = value + lax.dot_general(low, route, over, preferred_element_type=F32)
        state[:, v * 256 : v * 256 + 256] = value[0:200]

    high, low = split(state[...])
    inner[...] = dot(pick[...], high) + dot(pick[...], low)
    flat[...] = jnp.zeros_like(flat)
    for f in range(6):
        for v in range(5):
            flat[v * 25 : v * 25 + 25, f * 256 : f * 256 + 256] = inner[
                f * 32 : f * 32 + 25, v * 256 : v * 256 + 256
            ]
    high, low = split(flat[...])
    table[0:128, 0:1536] = high
    table[128:256, 0:1536] = low
    copies = []
    for k, (index_ref, steps) in enumerate(((up_ref, 1), (down_ref, -1))):
        got = dot(table[:, 0:1536], one_hot(index_ref[...], 6))
        sending[k] = got[0:128] + got[128:256]
        copy = pltpu.make_async_remote_copy(
            src_ref=sending.at[k],
            dst_ref=halo.at[k],
            send_sem=send_sem.at[4 + k],
            recv_sem=recv_sem.at[4 + k],
            device_id=place(steps),
            device_id_type=MESH,
        )
        copy.start()
        copies.append(copy)

    values = [state[:, v * 256 : v * 256 + 256] for v in range(5)]
    for i in range(3):
        n = [rows_of[i, :, :, j * 256 : j * 256 + 256].reshape(200, 256) for j in range(3)]
        along = n[0] * values[1] + n[1] * values[2] + n[2] * values[3]
        carried = mean_flow[0] * n[0] + mean_flow[1] * n[1] + mean_flow[2] * n[2]
        parts = [carried * values[0] + along]
        parts += [carried * values[1 + j] + n[j] * values[4] for j in range(3)]
        parts.append(carried * values[4] + along)
        for v in range(5):
            high, low = split(parts[v])
            flux_hi[i, :, v * 256 : v * 256 + 256] = high
            flux_lo[i, :, v * 256 : v * 256 + 256] = low
    gathered = None
    for i in range(3):
        cut = slice(i * 200, i * 200 + 200)
        term = (
            dot(slope_hi[:, cut], flux_hi[i])
            + dot(slope_hi[:, cut], flux_lo[i])
            + dot(slope_lo[:, cut], flux_hi[i])
        )
        gathered = term if gathered is None else gathered + term
    volume[...] = gathered

    for k, copy in enumerate(copies):
        copy.wait()
        real = rank > 0 if k == 0 else rank < total - 1
        high, low = split(jnp.where(real, halo[k], 0.0))
        table[0:128, 1536 + k * 256 : 1792 + k * 256] = high
        table[128:256, 1536 + k * 256 : 1792 + k * 256] = low

    def one_face(f, carry):
        links = near_ref[f]
        kind = kind_ref[pl.ds(f, 1), :]
        g = [
            dot(table[...], one_hot(links[q : q + 1, :], 8)).astype(BF16) for q in range(4)
        ]
        fine = dot(mortar_hi[0:960, :], g[0]) + dot(mortar_lo[0:960, :], g[0][0:128])
        coarse = fine[800:960]
        for q in range(1, 4):
            cut = slice(800 + q * 160, 960 + q * 160)
            coarse = coarse + dot(mortar_hi[cut, :], g[q]) + dot(mortar_lo[cut, :], g[q][0:128])
        outer = jnp.where(kind == 5, coarse, fine[0:160])
        for k in range(1, 5):
            outer = jnp.where(kind == k, fine[k * 160 : k * 160 + 160], outer)
        top = pl.multiple_of(f * 32, 32)
        side = jnp.where(lax.rem(f, 2) == 1, 1.0, -1.0)
        n = [normal[pl.ds(top, 32), j * 256 : j * 256 + 256] * side for j in range(3)]
        d = [
            outer[v * 32 : v * 32 + 32] - inner[pl.ds(top, 32), v * 256 : v * 256 + 256]
            for v in range(5)
        ]
        speed = speed_bound * (jnp.abs(n[0]) + jnp.abs(n[1]) + jnp.abs(n[2]))
        along = n[0] * d[1] + n[1] * d[2] + n[2] * d[3]
        excess = mean_flow[0] * n[0] + mean_flow[1] * n[1] + mean_flow[2] * n[2] - speed
        parts = [excess * d[0] + along]
        parts += [excess * d[1 + j] + n[j] * d[4] for j in range(3)]
        parts.append(excess * d[4] + along)
        for v in range(5):
            lift[pl.ds(top, 32), v * 256 : v * 256 + 256] = (0.5 * lift_scale) * parts[v]
        return carry

    lax.fori_loop(0, 6, one_face, 0)

    high, low = split(lift[...])
    result = volume[...] + dot(pick_t[...], high) + dot(pick_t[...], low)
    for v in range(5):
        piece = result[:, v * 256 : v * 256 + 256].reshape(25, 8, 256)[:, 0:5, :]
        out_ref[v * 25 : v * 25 + 25] = -jac_ref[...] * piece


def local(
    sizes, coeffs, refine_flag, new_owner, inv_jac, metric, neighbor, mortar, export_up, export_down
):
    constants, lift_scale = operators()
    count = coeffs.shape[-1]
    elements = inv_jac.shape[-1]
    operands = (
        coeffs.reshape(125, 5, count),
        refine_flag.reshape(1, count),
        new_owner.reshape(1, count),
        inv_jac.reshape(25, 5, elements),
        jnp.transpose(metric, (0, 2, 3, 4, 1, 5)).reshape(75, 5, 3, elements),
        jnp.transpose(neighbor, (1, 0, 2)),
        mortar,
        export_up.reshape(1, elements),
        export_down.reshape(1, elements),
    ) + tuple(jnp.asarray(c) for c in constants)
    vmem = pl.BlockSpec(memory_space=pltpu.VMEM)
    out = pl.pallas_call(
        functools.partial(body, sizes, lift_scale),
        out_shape=jax.ShapeDtypeStruct((125, 5, elements), F32),
        in_specs=[vmem] * len(operands),
        out_specs=vmem,
        scratch_shapes=[
            pltpu.VMEM((1280, count), F32),
            pltpu.VMEM((4, 8, 1408), F32),
            pltpu.VMEM((4, 8, 1408), F32),
            pltpu.VMEM((200, 1280), F32),
            pltpu.VMEM((3, 25, 8, 768), F32),
            pltpu.VMEM((3, 200, 1280), BF16),
            pltpu.VMEM((3, 200, 1280), BF16),
            pltpu.VMEM((200, 1280), F32),
            pltpu.VMEM((192, 1280), F32),
            pltpu.VMEM((192, 768), F32),
            pltpu.VMEM((128, 1536), F32),
            pltpu.VMEM((256, 2048), BF16),
            pltpu.VMEM((2, 128, 256), F32),
            pltpu.VMEM((2, 128, 256), F32),
            pltpu.VMEM((192, 1280), F32),
            pltpu.SemaphoreType.DMA((6,)),
            pltpu.SemaphoreType.DMA((6,)),
        ],
        compiler_params=pltpu.CompilerParams(
            collective_id=0, has_side_effects=True, vmem_limit_bytes=56 * 2**20
        ),
    )(*operands)
    return out.reshape(5, 5, 5, 5, elements)


def solution(mesh):
    sizes = tuple(mesh.shape[axis] for axis in AXES)
    in_specs = (
        P(None, None, None, None, AXES),
        P(AXES),
        P(AXES),
        P(None, None, None, AXES),
        P(None, None, None, None, None, AXES),
        P(None, None, AXES),
        P(None, AXES),
        P(AXES),
        P(AXES),
    )
    return jax.shard_map(
        functools.partial(local, sizes),
        mesh=mesh,
        in_specs=in_specs,
        out_specs=P(None, None, None, None, AXES),
        check_vma=False,
    )
```

time: 399 us -> 37.1 us (0.09)
  the two profiles are of different devices: /device:TPU:24 before, /device:TPU:0 now
where the time goes in v1:
time: 37.1 us; the launch traced here: 37 us
  Pallas kernels  34.7 us (94%)
  local copies, waits for them, and re-layouts  2.24 us (6%)
    pallas_call x1, Pallas kernels, local(): pl.pallas_call(functools.partial(body, sizes, lift_scale), out_shape=jax....  34.7 us
    unnamed x1, local copies, waits for them, and re-layouts  2.24 us

profile of v1, /device:TPU:0, one launch (start us, length us, event | category | flops | bytes accessed | tf_op | source)
XLA Modules:
  0.0 37.0 jit_solution(1169041878042123780)
XLA Ops:
  0.0 34.7 %shard_map.163 = f32[125,5,256]{2,1,0:T(8,128)} custom-call(f32[125,5,16]{2,1,0:T(8,128)} %bitcast.13, s32[1,16]{1,0:T(1,128)} %bitcast.18, s32[1,16]{1,0:T(1,128)} %bitcast.19, f32[25,5,256]{2,1,0:T(8,128)} %bitcast.14, f32[75,5,3,256]{3,2,1,0:T(4,128)} %bitcast.12, s32[6,4,256]{2,1,0:T(4,128)} %bitcast.15, s32[6,256]{1,0:T(8,128)} %kind_ref.1, ...), custom_call_target="tpu_custom_call" | custom-call | tf_op jit(solution)/shard_map/pallas_call | solution.py:411
  34.7 2.2 %copy.19 = f32[5,5,5,5,256]{4,3,2,1,0:T(8,128)} copy(f32[5,5,5,5,256]{4,3,2,1,0:T(8,128)} %bitcast.11) | data formatting | bytes 1280000

commit v2 on v1

--- a/solution.py
+++ b/solution.py
@@ -144,12 +144,13 @@
 
 def one_hot(index, chunks):
     count = index.shape[1]
-    rows = lax.broadcasted_iota(jnp.int32, (256, count), 0)
+    rows = lax.broadcasted_iota(jnp.int32, (256, count), 0).astype(F32).astype(BF16)
+    part, low = index >> 8, (index & 255).astype(F32)
+    one, zero = jnp.ones((), BF16), jnp.zeros((), BF16)
     parts = []
     for chunk in range(chunks):
-        parts.append(
-            jnp.where(rows == index - chunk * 256, 1.0, 0.0).astype(BF16)
-        )
+        here = jnp.where(part == chunk, low, -1.0).astype(BF16)
+        parts.append(jnp.where(rows == here, one, zero))
     return jnp.concatenate(parts, axis=0)
 
 
@@ -159,39 +160,34 @@
     coeffs_ref,
     flag_ref,
     owner_ref,
-    jac_ref,
-    metric_ref,
     near_ref,
     kind_ref,
     up_ref,
     down_ref,
-    refine_hi,
-    refine_lo,
-    slope_hi,
-    slope_lo,
     pick,
-    pick_t,
-    mortar_hi,
-    mortar_lo,
-    out_ref,
-    packed,
-    leaving,
-    arriving,
-    state,
-    rows_of,
-    flux_hi,
-    flux_lo,
-    volume,
-    inner,
-    normal,
-    flat,
-    table,
-    sending,
-    halo,
-    lift,
-    send_sem,
-    recv_sem,
+    *rest,
 ):
+    late, out_ref, late_here = rest[0:9], rest[9], rest[10:19]
+    (
+        packed,
+        leaving,
+        arriving,
+        state,
+        rows_of,
+        flux_hi,
+        flux_lo,
+        volume,
+        inner,
+        normal,
+        flat,
+        table,
+        sending,
+        halo,
+        lift,
+        send_sem,
+        recv_sem,
+        load_sem,
+    ) = rest[19:]
     nx, ny, nz = sizes
     total = nx * ny * nz
     rank = (lax.axis_index("gx") * ny + lax.axis_index("gy")) * nz + lax.axis_index("gz")
@@ -200,9 +196,22 @@
         other = lax.rem(rank + steps + total, total)
         return (other // (ny * nz), lax.rem(other // nz, ny), lax.rem(other, nz))
 
+    def there(steps):
+        return (rank + steps >= 0) & (rank + steps < total)
+
     barrier = pltpu.get_barrier_semaphore()
     for steps in band_steps:
-        pl.semaphore_signal(barrier, inc=1, device_id=place(steps), device_id_type=MESH)
+
+        @pl.when(there(steps))
+        def _(steps=steps):
+            pl.semaphore_signal(barrier, inc=1, device_id=place(steps), device_id_type=MESH)
+
+    loads = []
+    for number, (source, target) in enumerate(zip(late, late_here)):
+        load = pltpu.make_async_copy(source, target, load_sem.at[number])
+        load.start()
+        loads.append(load)
+    metric_ref, refine_hi, refine_lo, slope_hi, slope_lo, pick_t, mortar_hi, mortar_lo, jac_ref = late_here
 
     count = coeffs_ref.shape[-1]
     packed[...] = jnp.zeros_like(packed)
@@ -237,7 +246,8 @@
         leaving[k, :, 0:1280] = placed[k * 8 : k * 8 + 8]
         leaving[k, :, 1280:1408] = flags[k * 8 : k * 8 + 8]
 
-    pl.semaphore_wait(barrier, 4)
+    around = sum(there(steps).astype(jnp.int32) for steps in band_steps)
+    pl.semaphore_wait(barrier, around)
     moves = []
     for k in range(4):
         move = pltpu.make_async_remote_copy(
@@ -248,8 +258,14 @@
             device_id=place(band_steps[k]),
             device_id_type=MESH,
         )
-        move.start()
+        pl.when(there(band_steps[k]))(move.start)
         moves.append(move)
+
+        @pl.when(jnp.logical_not(there(-band_steps[k])))
+        def _(k=k):
+            arriving[k] = jnp.zeros_like(arriving[k])
+
+    loads[0].wait()
 
     rows_of[...] = jnp.zeros_like(rows_of)
     for i in range(3):
@@ -261,8 +277,10 @@
         high, low = split(rows_of[i].reshape(200, 768))
         faces = pick[i * 64 : i * 64 + 64, :]
         normal[i * 64 : i * 64 + 64, :] = dot(faces, high) + dot(faces, low)
-    for move in moves:
-        move.wait()
+    loads[1].wait()
+    loads[2].wait()
+    for k, move in enumerate(moves):
+        pl.when(there(-band_steps[k]))(move.wait_recv)
 
     parents = [
         jnp.concatenate(
@@ -317,8 +335,15 @@
             device_id=place(steps),
             device_id_type=MESH,
         )
-        copy.start()
-        copies.append(copy)
+        pl.when(there(steps))(copy.start)
+        copies.append((copy, steps))
+
+        @pl.when(jnp.logical_not(there(-steps)))
+        def _(k=k):
+            halo[k] = jnp.zeros_like(halo[k])
+
+    loads[3].wait()
+    loads[4].wait()
 
     values = [state[:, v * 256 : v * 256 + 256] for v in range(5)]
     for i in range(3):
@@ -343,12 +368,14 @@
         gathered = term if gathered is None else gathered + term
     volume[...] = gathered
 
-    for k, copy in enumerate(copies):
-        copy.wait()
-        real = rank > 0 if k == 0 else rank < total - 1
-        high, low = split(jnp.where(real, halo[k], 0.0))
+    for k, (copy, steps) in enumerate(copies):
+        pl.when(there(-steps))(copy.wait_recv)
+        high, low = split(halo[k])
         table[0:128, 1536 + k * 256 : 1792 + k * 256] = high
         table[128:256, 1536 + k * 256 : 1792 + k * 256] = low
+
+    for load in loads[5:]:
+        load.wait()
 
     def one_face(f, carry):
         links = near_ref[f]
@@ -383,6 +410,10 @@
 
     lax.fori_loop(0, 6, one_face, 0)
 
+    for k, move in enumerate(moves):
+        pl.when(there(band_steps[k]))(move.wait_send)
+    for copy, steps in copies:
+        pl.when(there(steps))(copy.wait_send)
     high, low = split(lift[...])
     result = volume[...] + dot(pick_t[...], high) + dot(pick_t[...], low)
     for v in range(5):
@@ -396,24 +427,30 @@
     constants, lift_scale = operators()
     count = coeffs.shape[-1]
     elements = inv_jac.shape[-1]
-    operands = (
+    refine_hi, refine_lo, slope_hi, slope_lo, pick, pick_t, mortar_hi, mortar_lo = (
+        jnp.asarray(c) for c in constants
+    )
+    rows = jnp.transpose(metric, (0, 2, 3, 4, 1, 5)).reshape(75, 5, 3, elements)
+    jac = inv_jac.reshape(25, 5, elements)
+    early = (
         coeffs.reshape(125, 5, count),
         refine_flag.reshape(1, count),
         new_owner.reshape(1, count),
-        inv_jac.reshape(25, 5, elements),
-        jnp.transpose(metric, (0, 2, 3, 4, 1, 5)).reshape(75, 5, 3, elements),
         jnp.transpose(neighbor, (1, 0, 2)),
         mortar,
         export_up.reshape(1, elements),
         export_down.reshape(1, elements),
-    ) + tuple(jnp.asarray(c) for c in constants)
+        pick,
+    )
+    late = (rows, refine_hi, refine_lo, slope_hi, slope_lo, pick_t, mortar_hi, mortar_lo, jac)
     vmem = pl.BlockSpec(memory_space=pltpu.VMEM)
     out = pl.pallas_call(
         functools.partial(body, sizes, lift_scale),
         out_shape=jax.ShapeDtypeStruct((125, 5, elements), F32),
-        in_specs=[vmem] * len(operands),
+        in_specs=[vmem] * len(early) + [pl.BlockSpec(memory_space=pl.ANY)] * len(late),
         out_specs=vmem,
-        scratch_shapes=[
+        scratch_shapes=[pltpu.VMEM(x.shape, x.dtype) for x in late]
+        + [
             pltpu.VMEM((1280, count), F32),
             pltpu.VMEM((4, 8, 1408), F32),
             pltpu.VMEM((4, 8, 1408), F32),
@@ -431,11 +468,12 @@
             pltpu.VMEM((192, 1280), F32),
             pltpu.SemaphoreType.DMA((6,)),
             pltpu.SemaphoreType.DMA((6,)),
+            pltpu.SemaphoreType.DMA((9,)),
         ],
         compiler_params=pltpu.CompilerParams(
             collective_id=0, has_side_effects=True, vmem_limit_bytes=56 * 2**20
         ),
-    )(*operands)
+    )(*early, *late)
     return out.reshape(5, 5, 5, 5, elements)
 
 

time: 37.1 us -> 31.3 us (0.84)
  the two profiles are of different devices: /device:TPU:0 before, /device:TPU:1 now
where the time goes in v2:
time: 31.3 us; the launch traced here: 31.1 us
  Pallas kernels  28.9 us (92%)
  local copies, waits for them, and re-layouts  2.24 us (7%)
    pallas_call x1, Pallas kernels, local(): pl.pallas_call(functools.partial(body, sizes, lift_scale), out_shape=jax....  28.9 us
    unnamed x1, local copies, waits for them, and re-layouts  2.24 us

profile of v2, /device:TPU:1, one launch (start us, length us, event | category | flops | bytes accessed | tf_op | source)
XLA Modules:
  0.0 31.1 jit_solution(10342469622482219732)
XLA Ops:
  0.0 28.9 %shard_map.163 = f32[125,5,256]{2,1,0:T(8,128)} custom-call(f32[125,5,16]{2,1,0:T(8,128)} %bitcast.13, s32[1,16]{1,0:T(1,128)} %bitcast.18, s32[1,16]{1,0:T(1,128)} %bitcast.19, s32[6,4,256]{2,1,0:T(4,128)} %bitcast.15, s32[6,256]{1,0:T(8,128)} %kind_ref.1, s32[1,256]{1,0:T(1,128)} %bitcast.16, s32[1,256]{1,0:T(1,128)} %bitcast.17, ...), custom_call_target="tpu_custom_call" | custom-call | tf_op jit(solution)/shard_map/pallas_call | solution.py:447
  28.9 2.2 %copy.19 = f32[5,5,5,5,256]{4,3,2,1,0:T(8,128)} copy(f32[5,5,5,5,256]{4,3,2,1,0:T(8,128)} %bitcast.11) | data formatting | bytes 1280000

commit v3 on v2

--- a/solution.py
+++ b/solution.py
@@ -184,6 +184,7 @@
         sending,
         halo,
         lift,
+        fetched,
         send_sem,
         recv_sem,
         load_sem,
@@ -233,13 +234,11 @@
     chosen = jnp.where(
         lax.broadcasted_iota(jnp.int32, (slots, count), 0) == spot, 1.0, 0.0
     ).astype(F32)
-    placed = lax.dot_general(
-        chosen,
-        packed[...],
-        (((1,), (1,)), ((), ())),
-        precision=lax.Precision.HIGHEST,
-        preferred_element_type=F32,
-    )
+    along_lanes = (((1,), (1,)), ((), ()))
+    high, low = split(packed[...])
+    picked = chosen.astype(BF16)
+    placed = lax.dot_general(picked, high, along_lanes, preferred_element_type=F32)
+    placed = placed + lax.dot_general(picked, low, along_lanes, preferred_element_type=F32)
     flags = jnp.sum(chosen * flag_ref[...].astype(F32), axis=1, keepdims=True)
     flags = jnp.broadcast_to(flags, (slots, 128))
     for k in range(4):
@@ -368,6 +367,15 @@
         gathered = term if gathered is None else gathered + term
     volume[...] = gathered
 
+    def own_part(f, carry):
+        links = near_ref[f]
+        for q in range(4):
+            got = dot(table[:, 0:1536], one_hot(links[q : q + 1, :], 6))
+            fetched[f, :, q * 256 : q * 256 + 256] = got.astype(BF16)
+        return carry
+
+    lax.fori_loop(0, 6, own_part, 0)
+
     for k, (copy, steps) in enumerate(copies):
         pl.when(there(-steps))(copy.wait_recv)
         high, low = split(halo[k])
@@ -381,7 +389,9 @@
         links = near_ref[f]
         kind = kind_ref[pl.ds(f, 1), :]
         g = [
-            dot(table[...], one_hot(links[q : q + 1, :], 8)).astype(BF16) for q in range(4)
+            fetched[f, :, q * 256 : q * 256 + 256]
+            + dot(table[:, 1536:2048], one_hot(links[q : q + 1, :] - 1536, 2)).astype(BF16)
+            for q in range(4)
         ]
         fine = dot(mortar_hi[0:960, :], g[0]) + dot(mortar_lo[0:960, :], g[0][0:128])
         coarse = fine[800:960]
@@ -466,6 +476,7 @@
             pltpu.VMEM((2, 128, 256), F32),
             pltpu.VMEM((2, 128, 256), F32),
             pltpu.VMEM((192, 1280), F32),
+            pltpu.VMEM((6, 256, 1024), BF16),
             pltpu.SemaphoreType.DMA((6,)),
             pltpu.SemaphoreType.DMA((6,)),
             pltpu.SemaphoreType.DMA((9,)),

time: 31.3 us -> 30.3 us (0.968)
  the two profiles are of different devices: /device:TPU:1 before, /device:TPU:0 now
where the time goes in v3:
time: 30.3 us; the launch traced here: 30.1 us
  Pallas kernels  27.9 us (92%)
  local copies, waits for them, and re-layouts  2.24 us (7%)
    pallas_call x1, Pallas kernels, local(): pl.pallas_call(functools.partial(body, sizes, lift_scale), out_shape=jax....  27.9 us
    unnamed x1, local copies, waits for them, and re-layouts  2.24 us

profile of v3, /device:TPU:0, one launch (start us, length us, event | category | flops | bytes accessed | tf_op | source)
XLA Modules:
  0.0 30.1 jit_solution(5197314723482419917)
XLA Ops:
  0.0 27.9 %shard_map.163 = f32[125,5,256]{2,1,0:T(8,128)} custom-call(f32[125,5,16]{2,1,0:T(8,128)} %bitcast.13, s32[1,16]{1,0:T(1,128)} %bitcast.18, s32[1,16]{1,0:T(1,128)} %bitcast.19, s32[6,4,256]{2,1,0:T(4,128)} %bitcast.15, s32[6,256]{1,0:T(8,128)} %kind_ref.1, s32[1,256]{1,0:T(1,128)} %bitcast.16, s32[1,256]{1,0:T(1,128)} %bitcast.17, ...), custom_call_target="tpu_custom_call" | custom-call | tf_op jit(solution)/shard_map/pallas_call | solution.py:457
  27.9 2.2 %copy.19 = f32[5,5,5,5,256]{4,3,2,1,0:T(8,128)} copy(f32[5,5,5,5,256]{4,3,2,1,0:T(8,128)} %bitcast.11) | data formatting | bytes 1280000
